TPU v7x, 128 devices: a whole 4x4x4 slice. The times are simulated.
128 devices in a mesh: tile: 32 (over x, y, core), lev: 4 (over z).
Axes of the slice: x: 4, y: 4, z: 4, core: 2. Of those that a mesh axis runs over, the one named last changes fastest.
Arguments:
- state: float32 [32, 80, 16384], P('lev', None, 'tile'), may hold values from -6 to 6
- obs_prior: float32 [8, 80, 2048], P(None, None, ('tile', 'lev')), may hold values from -6 to 6
- obs_value: float32 [8, 2048], P(None, ('tile', 'lev')), may hold values from -8 to 8
- obs_error: float32 [8, 2048], P(None, ('tile', 'lev')), may hold values from 0.3 to 3
- obs_place: float32 [8, 2048], P(None, ('tile', 'lev')), may hold values from 0 to 1
- obs_height: float32 [8, 2048], P(None, ('tile', 'lev')), may hold values from 0 to 32
- tile_blocks: int32 [8, 32, 6], P(None, 'tile'), may hold values from 0 to 15, as said below
- tile_counts: int32 [8, 32], P(None, 'tile'), may hold values from 1 to 6, as said below
- loc_blocks: bfloat16 [8, 768, 16384], P(None, None, 'tile'), may hold values from 0.19921875 to 1
- pair_mask: int32 [8, 16, 8, 16], replicated, may hold values 0 or 1
Outputs:
- analysis: float32 [32, 80, 16384], P('lev', None, 'tile')
- obs_post: float32 [8, 80, 2048], P(None, None, ('tile', 'lev'))
Inputs may be any that keep to these rules, and one draw needn't show every extreme that they name: `tile_blocks`: each row lists 6 different blocks. `tile_counts`: in every batch some tile uses all 6 of its blocks.
All inputs are finite; a program needn't handle non-finite values.
Results may differ from a plain program's by a relative error of at most 0.035.
Values may be sent and summed in bfloat16 or wider, within the bound.
A program may use at most 128 MiB of HBM per device.

v0:
```python
import math

import jax
import jax.numpy as jnp
from jax import lax
from jax.sharding import PartitionSpec as P

K = 80
NB = 8
B = 2048
OBLK = 128
MAXB = 6
NOB = 16


EPS = 1e-05
REACH = 0.25


def closeness(gap, reach):
    return 1.0 / (1.0 + (gap / reach) ** 2)


def pick_blocks(values, block_ids):
    shaped = values.reshape(values.shape[:-1] + (NOB, OBLK))
    chosen = jnp.take(shaped, block_ids, axis=values.ndim - 1)
    return chosen.reshape(values.shape[:-1] + (MAXB * OBLK,))


def tile_update(
    column_block,
    block_ids,
    used_count,
    locality,
    anomaly_low,
    delta_low,
    variance,
    height_row,
    level_pos,
    vreach,
):
    chosen_anom = pick_blocks(anomaly_low, block_ids)
    chosen_delta = pick_blocks(delta_low, block_ids)
    chosen_var = pick_blocks(variance, block_ids)
    chosen_height = pick_blocks(height_row, block_ids)
    valid = jnp.repeat((jnp.arange(MAXB) < used_count).astype(jnp.float32), OBLK)
    average = jnp.mean(column_block, axis=1, keepdims=True)
    state_low = (column_block - average).astype(jnp.bfloat16)
    covar = jnp.einsum(
        "km,lkc->lmc", chosen_anom, state_low, preferred_element_type=jnp.float32
    ) / (K - 1)
    vertical = closeness(level_pos[:, None] - chosen_height[None, :], vreach)
    scaling = vertical * (valid * (4.0 / math.sqrt(MAXB * OBLK)) / chosen_var)[None, :]
    gain_low = (covar * scaling[:, :, None] * locality.astype(jnp.float32)[None]).astype(
        jnp.bfloat16
    )
    return column_block + jnp.einsum(
        "km,lmc->lkc", chosen_delta, gain_low, preferred_element_type=jnp.float32
    )


def per_device(
    state,
    obs_prior,
    obs_value,
    obs_error,
    obs_place,
    obs_height,
    tile_blocks,
    tile_counts,
    loc_blocks,
    pair_mask,
):
    level_count = state.shape[0]
    own_count = obs_prior.shape[2]
    vreach = level_count * lax.axis_size("lev") / 4.0
    couple = 4.0 / math.sqrt(B)
    place_all, height_all = (
        lax.all_gather(obs_place, ("tile", "lev"), axis=1, tiled=True),
        lax.all_gather(obs_height, ("tile", "lev"), axis=1, tiled=True),
    )
    first_obs = lax.axis_index(("tile", "lev")) * own_count
    own_blocks = (first_obs + jnp.arange(own_count)) // OBLK
    level_pos = (lax.axis_index("lev") * level_count + jnp.arange(level_count)).astype(
        jnp.float32
    ) + 0.5
    prior_list = [obs_prior[batch_id] for batch_id in range(NB)]
    analysis = state
    for batch_id in range(NB):
        current = prior_list[batch_id]
        average = jnp.mean(current, axis=0)
        anomaly = current - average
        variance = jnp.sum(anomaly * anomaly, axis=0) / (K - 1) + EPS
        mismatch = obs_value[batch_id] - average
        obs_err = obs_error[batch_id]
        total_miss, total_spread = lax.psum(
            (jnp.sum(mismatch * mismatch), jnp.sum(variance + obs_err)), ("tile", "lev")
        )
        gamma_sq = total_miss / total_spread
        inflated = gamma_sq * variance
        increment = inflated / (inflated + obs_err) * mismatch
        factor = jnp.sqrt(gamma_sq * obs_err / (inflated + obs_err)) - 1.0
        anomaly_low = anomaly.astype(jnp.bfloat16)
        delta_low = (increment + factor * anomaly_low.astype(jnp.float32)).astype(jnp.bfloat16)
        prior_list[batch_id] = current + delta_low.astype(jnp.float32)
        anom_all, delta_all, var_all = (
            lax.all_gather(anomaly_low, ("tile", "lev"), axis=1, tiled=True),
            lax.all_gather(delta_low, ("tile", "lev"), axis=1, tiled=True),
            lax.all_gather(
                variance.astype(jnp.bfloat16), ("tile", "lev"), axis=0, tiled=True
            ).astype(variance.dtype),
        )
        for later_id in range(batch_id + 1, NB):
            other_obs = prior_list[later_id]
            other_low = (other_obs - jnp.mean(other_obs, axis=0)).astype(jnp.bfloat16)
            covar = lax.dot_general(
                other_low, anom_all, (((0,), (0,)), ((), ())), preferred_element_type=jnp.float32
            ) / (K - 1)
            block_mask = jnp.repeat(
                jnp.take(pair_mask[later_id, :, batch_id, :], own_blocks, axis=0), OBLK, axis=1
            ).astype(jnp.float32)
            locality = block_mask * closeness(
                obs_place[later_id][:, None] - place_all[batch_id][None, :], REACH
            )
            gain_low = (covar * locality * couple / var_all[None, :]).astype(jnp.bfloat16)
            prior_list[later_id] = other_obs + lax.dot_general(
                delta_all, gain_low, (((1,), (1,)), ((), ())), preferred_element_type=jnp.float32
            )
        analysis = tile_update(
            analysis,
            tile_blocks[batch_id, 0],
            tile_counts[batch_id, 0],
            loc_blocks[batch_id],
            anom_all,
            delta_all,
            var_all,
            height_all[batch_id],
            level_pos,
            vreach,
        )
    return (analysis, jnp.stack(prior_list))


def solution(mesh):
    placed = (
        P("lev", None, "tile"),
        P(None, None, ("tile", "lev")),
        P(None, ("tile", "lev")),
        P(None, ("tile", "lev")),
        P(None, ("tile", "lev")),
        P(None, ("tile", "lev")),
        P(None, "tile", None),
        P(None, "tile"),
        P(None, None, "tile"),
        P(),
    )
    return jax.shard_map(
        per_device,
        mesh=mesh,
        in_specs=placed,
        out_specs=(P("lev", None, "tile"), P(None, None, ("tile", "lev"))),
        check_vma=False,
    )
```

profile of v0, /device:TPU:0, one launch (start us, length us, event | category | flops | bytes accessed | tf_op | source)
XLA Modules:
  0.0 2244.9 jit_solution(5655173848417837729)
XLA Ops:
  11.8 68.2 %all-reduce.15 = (f32[]{:T(128)}, f32[]{:T(128)}) all-reduce(f32[]{:T(128)} %get-tuple-element.255, f32[]{:T(128)} %get-tuple-element.253), channel_id=1, replica_groups=mesh['tile'=32,'lev'=4] {'tile','lev'}, use_global_device_ids=true, to_apply=%region_4.0 | all-reduce | flops 2 | bytes 16 | tf_op jit(solution)/shard_map/psum | solution.py:96
  182.7 64.8 %all-reduce = bf16[2048]{0:T(1024)(128)(2,1)S(1)} all-reduce(bf16[2048]{0:T(1024)(128)(2,1)S(1)} %dynamic-update-slice), channel_id=1, replica_groups=mesh['tile'=32,'lev'=4] {'tile','lev'}, use_global_device_ids=true, to_apply=%add | all-reduce | flops 2048 | bytes 8192
  301.0 64.7 %all-reduce.14 = (f32[]{:T(128)}, f32[]{:T(128)}) all-reduce(f32[]{:T(128)} %get-tuple-element.247, f32[]{:T(128)} %get-tuple-element.245), channel_id=1, replica_groups=mesh['tile'=32,'lev'=4] {'tile','lev'}, use_global_device_ids=true, to_apply=%region_12.0 | all-reduce | flops 2 | bytes 16 | tf_op jit(solution)/shard_map/psum | solution.py:96
  468.6 64.9 %all-reduce.1 = bf16[2048]{0:T(1024)(128)(2,1)S(1)} all-reduce(bf16[2048]{0:T(1024)(128)(2,1)S(1)} %dynamic-update-slice.1), channel_id=1, replica_groups=mesh['tile'=32,'lev'=4] {'tile','lev'}, use_global_device_ids=true, to_apply=%add.1 | all-reduce | flops 2048 | bytes 8192
  550.6 63.2 %all-reduce.13 = (f32[]{:T(128)}, f32[]{:T(128)}) all-reduce(f32[]{:T(128)} %get-tuple-element.239, f32[]{:T(128)} %get-tuple-element.237), channel_id=1, replica_groups=mesh['tile'=32,'lev'=4] {'tile','lev'}, use_global_device_ids=true, to_apply=%region_21.25 | all-reduce | flops 2 | bytes 16 | tf_op jit(solution)/shard_map/psum | solution.py:96
  716.5 64.8 %all-reduce.2 = bf16[2048]{0:T(1024)(128)(2,1)S(1)} all-reduce(bf16[2048]{0:T(1024)(128)(2,1)S(1)} %dynamic-update-slice.2), channel_id=1, replica_groups=mesh['tile'=32,'lev'=4] {'tile','lev'}, use_global_device_ids=true, to_apply=%add.2 | all-reduce | flops 2048 | bytes 8192
  792.4 63.2 %all-reduce.12 = (f32[]{:T(128)}, f32[]{:T(128)}) all-reduce(f32[]{:T(128)} %get-tuple-element.231, f32[]{:T(128)} %get-tuple-element.229), channel_id=1, replica_groups=mesh['tile'=32,'lev'=4] {'tile','lev'}, use_global_device_ids=true, to_apply=%region_31.35 | all-reduce | flops 2 | bytes 16 | tf_op jit(solution)/shard_map/psum | solution.py:96
  857.5 52.9 %all_gather.89 = bf16[80,2048]{0,1:T(8,128)(2,1)} all-gather(bf16[80,16]{0,1:T(8,128)(2,1)S(1)} %get-tuple-element.51), channel_id=1, replica_groups=mesh['tile'=32,'lev'=4] {'tile','lev'}, dimensions={1}, use_global_device_ids=true | all-gather | bytes 330240 | tf_op jit(solution)/shard_map/all_gather | solution.py:107
  910.4 54.3 %all_gather.91 = bf16[80,2048]{0,1:T(8,128)(2,1)} all-gather(bf16[80,16]{0,1:T(8,128)(2,1)S(1)} %get-tuple-element.50), channel_id=1, replica_groups=mesh['tile'=32,'lev'=4] {'tile','lev'}, dimensions={1}, use_global_device_ids=true | all-gather | bytes 330240 | tf_op jit(solution)/shard_map/all_gather | solution.py:108
  964.9 65.0 %all-reduce.3 = bf16[2048]{0:T(1024)(128)(2,1)S(1)} all-reduce(bf16[2048]{0:T(1024)(128)(2,1)S(1)} %dynamic-update-slice.3), channel_id=1, replica_groups=mesh['tile'=32,'lev'=4] {'tile','lev'}, use_global_device_ids=true, to_apply=%add.3 | all-reduce | flops 2048 | bytes 8192
  1046.4 63.9 %all-reduce.11 = (f32[]{:T(128)}, f32[]{:T(128)}) all-reduce(f32[]{:T(128)} %get-tuple-element.223, f32[]{:T(128)} %get-tuple-element.221), channel_id=1, replica_groups=mesh['tile'=32,'lev'=4] {'tile','lev'}, use_global_device_ids=true, to_apply=%region_42.46 | all-reduce | flops 2 | bytes 16 | tf_op jit(solution)/shard_map/psum | solution.py:96
  1112.4 52.8 %all_gather.92 = bf16[80,2048]{0,1:T(8,128)(2,1)} all-gather(bf16[80,16]{0,1:T(8,128)(2,1)S(1)} %get-tuple-element.48), channel_id=1, replica_groups=mesh['tile'=32,'lev'=4] {'tile','lev'}, dimensions={1}, use_global_device_ids=true | all-gather | bytes 330240 | tf_op jit(solution)/shard_map/all_gather | solution.py:107
  1165.2 54.3 %all_gather.94 = bf16[80,2048]{0,1:T(8,128)(2,1)} all-gather(bf16[80,16]{0,1:T(8,128)(2,1)S(1)} %get-tuple-element.47), channel_id=1, replica_groups=mesh['tile'=32,'lev'=4] {'tile','lev'}, dimensions={1}, use_global_device_ids=true | all-gather | bytes 330240 | tf_op jit(solution)/shard_map/all_gather | solution.py:108
  1219.7 64.8 %all-reduce.4 = bf16[2048]{0:T(1024)(128)(2,1)S(1)} all-reduce(bf16[2048]{0:T(1024)(128)(2,1)S(1)} %dynamic-update-slice.4), channel_id=1, replica_groups=mesh['tile'=32,'lev'=4] {'tile','lev'}, use_global_device_ids=true, to_apply=%add.4 | all-reduce | flops 2048 | bytes 8192
  1300.0 63.9 %all-reduce.10 = (f32[]{:T(128)}, f32[]{:T(128)}) all-reduce(f32[]{:T(128)} %get-tuple-element.215, f32[]{:T(128)} %get-tuple-element.213), channel_id=1, replica_groups=mesh['tile'=32,'lev'=4] {'tile','lev'}, use_global_device_ids=true, to_apply=%region_54.58 | all-reduce | flops 2 | bytes 16 | tf_op jit(solution)/shard_map/psum | solution.py:96
  1418.3 55.0 %all_gather.97 = bf16[80,2048]{0,1:T(8,128)(2,1)} all-gather(bf16[80,16]{0,1:T(8,128)(2,1)S(1)} %get-tuple-element.44), channel_id=1, replica_groups=mesh['tile'=32,'lev'=4] {'tile','lev'}, dimensions={1}, use_global_device_ids=true | all-gather | bytes 330240 | tf_op jit(solution)/shard_map/all_gather | solution.py:108
  1473.5 64.8 %all-reduce.5 = bf16[2048]{0:T(1024)(128)(2,1)S(1)} all-reduce(bf16[2048]{0:T(1024)(128)(2,1)S(1)} %dynamic-update-slice.5), channel_id=1, replica_groups=mesh['tile'=32,'lev'=4] {'tile','lev'}, use_global_device_ids=true, to_apply=%add.5 | all-reduce | flops 2048 | bytes 8192
  1541.6 63.9 %all-reduce.9 = (f32[]{:T(128)}, f32[]{:T(128)}) all-reduce(f32[]{:T(128)} %get-tuple-element.207, f32[]{:T(128)} %get-tuple-element.205), channel_id=1, replica_groups=mesh['tile'=32,'lev'=4] {'tile','lev'}, use_global_device_ids=true, to_apply=%region_67.71 | all-reduce | flops 2 | bytes 16 | tf_op jit(solution)/shard_map/psum | solution.py:96
  1607.5 52.8 %all_gather.100 = bf16[80,2048]{0,1:T(8,128)(2,1)} all-gather(bf16[80,16]{0,1:T(8,128)(2,1)S(1)} %get-tuple-element.41), channel_id=1, replica_groups=mesh['tile'=32,'lev'=4] {'tile','lev'}, dimensions={1}, use_global_device_ids=true | all-gather | bytes 330240 | tf_op jit(solution)/shard_map/all_gather | solution.py:108
  1660.4 54.3 %all_gather.98 = bf16[80,2048]{0,1:T(8,128)(2,1)} all-gather(bf16[80,16]{0,1:T(8,128)(2,1)S(1)} %get-tuple-element.42), channel_id=1, replica_groups=mesh['tile'=32,'lev'=4] {'tile','lev'}, dimensions={1}, use_global_device_ids=true | all-gather | bytes 330240 | tf_op jit(solution)/shard_map/all_gather | solution.py:107
  1714.9 64.8 %all-reduce.6 = bf16[2048]{0:T(1024)(128)(2,1)S(1)} all-reduce(bf16[2048]{0:T(1024)(128)(2,1)S(1)} %dynamic-update-slice.6), channel_id=1, replica_groups=mesh['tile'=32,'lev'=4] {'tile','lev'}, use_global_device_ids=true, to_apply=%add.6 | all-reduce | flops 2048 | bytes 8192
  1793.1 63.9 %all-reduce.8 = (f32[]{:T(128)}, f32[]{:T(128)}) all-reduce(f32[]{:T(128)} %get-tuple-element.171, f32[]{:T(128)} %get-tuple-element.169), channel_id=1, replica_groups=mesh['tile'=32,'lev'=4] {'tile','lev'}, use_global_device_ids=true, to_apply=%region_81.85 | all-reduce | flops 2 | bytes 16 | tf_op jit(solution)/shard_map/psum | solution.py:96
  1915.7 54.4 %all_gather.101 = bf16[80,2048]{0,1:T(8,128)(2,1)} all-gather(bf16[80,16]{0,1:T(8,128)(2,1)S(1)} %get-tuple-element.39), channel_id=1, replica_groups=mesh['tile'=32,'lev'=4] {'tile','lev'}, dimensions={1}, use_global_device_ids=true | all-gather | bytes 330240 | tf_op jit(solution)/shard_map/all_gather | solution.py:107
  2016.1 64.8 %all-reduce.7 = bf16[2048]{0:T(1024)(128)(2,1)S(1)} all-reduce(bf16[2048]{0:T(1024)(128)(2,1)S(1)} %dynamic-update-slice.7), channel_id=1, replica_groups=mesh['tile'=32,'lev'=4] {'tile','lev'}, use_global_device_ids=true, to_apply=%add.7 | all-reduce | flops 2048 | bytes 8192
  (496 shorter events, 767.4 us)
Async XLA Ops:
  0.7 246.8 %copy-start.23 = (f32[8,16]{1,0:T(8,128)S(1)}, f32[8,16]{1,0:T(8,128)}, u32[]{:S(2)}) copy-start(f32[8,16]{1,0:T(8,128)} %param.20) | copy-start | bytes 1540
  247.5 300.4 %copy-start.39 = (f32[2048]{0:T(1024)}, f32[2048]{0:T(1024)S(1)}, u32[]{:S(2)}) copy-start(f32[2048]{0:T(1024)S(1)} %get-tuple-element.146) | copy-start | bytes 24580
  298.4 249.5 %copy-start.36 = (f32[1,2048]{1,0:T(1,128)}, f32[1,2048]{1,0:T(1,128)S(1)}, u32[]{:S(2)}) copy-start(f32[1,2048]{1,0:T(1,128)S(1)} %get-tuple-element.110) | copy-start | bytes 24580
  298.4 250.1 %copy-start.32 = (f32[1,2048]{1,0:T(1,128)}, f32[1,2048]{1,0:T(1,128)S(1)}, u32[]{:S(2)}) copy-start(f32[1,2048]{1,0:T(1,128)S(1)} %get-tuple-element.109) | copy-start | bytes 24580
  299.0 246.6 %copy-start.65 = (f32[16]{0:T(128)}, f32[16]{0:T(128)S(1)}, u32[]{:S(2)}) copy-start(f32[16]{0:T(128)S(1)} %get-tuple-element.135) | copy-start | bytes 196
  789.6 241.0 %copy-start.27 = (f32[1,2048]{1,0:T(1,128)S(1)}, f32[1,2048]{1,0:T(1,128)}, u32[]{:S(2)}) copy-start(f32[1,2048]{1,0:T(1,128)} %get-tuple-element.107) | copy-start | bytes 24580
  1043.1 242.1 %copy-start.26 = (f32[1,2048]{1,0:T(1,128)S(1)}, f32[1,2048]{1,0:T(1,128)}, u32[]{:S(2)}) copy-start(f32[1,2048]{1,0:T(1,128)} %get-tuple-element.106) | copy-start | bytes 24580
  1112.4 175.9 %copy-start.37 = (f32[1,2048]{1,0:T(1,128)S(1)}, f32[1,2048]{1,0:T(1,128)}, u32[]{:S(2)}) copy-start(f32[1,2048]{1,0:T(1,128)} %copy-done.36) | copy-start | bytes 24580
  1296.7 241.8 %copy-start.25 = (f32[1,2048]{1,0:T(1,128)S(1)}, f32[1,2048]{1,0:T(1,128)}, u32[]{:S(2)}) copy-start(f32[1,2048]{1,0:T(1,128)} %get-tuple-element.105) | copy-start | bytes 24580
  1296.7 241.8 %copy-start.66 = (f32[16]{0:T(128)S(1)}, f32[16]{0:T(128)}, u32[]{:S(2)}) copy-start(f32[16]{0:T(128)} %copy-done.65) | copy-start | bytes 196
  1538.4 176.6 %copy-start.49 = (f32[2048]{0:T(1024)}, f32[2048]{0:T(1024)S(1)}, u32[]{:S(2)}) copy-start(f32[2048]{0:T(1024)S(1)} %get-tuple-element.136) | copy-start | bytes 24580
  1538.4 241.5 %copy-start.38 = (f32[1,2048]{1,0:T(1,128)S(1)}, f32[1,2048]{1,0:T(1,128)}, u32[]{:S(2)}) copy-start(f32[1,2048]{1,0:T(1,128)} %copy-done.36) | copy-start | bytes 24580
  1538.4 241.5 %copy-start.40 = (f32[2048]{0:T(1024)S(1)}, f32[2048]{0:T(1024)}, u32[]{:S(2)}) copy-start(f32[2048]{0:T(1024)} %copy-done.39) | copy-start | bytes 24580
  1606.8 174.9 %copy-start.35 = (f32[1,2048]{1,0:T(1,128)S(1)}, f32[1,2048]{1,0:T(1,128)}, u32[]{:S(2)}) copy-start(f32[1,2048]{1,0:T(1,128)} %copy-done.32) | copy-start | bytes 24580
  1606.8 174.9 %copy-start.44 = (f32[2048]{0:T(1024)S(1)}, f32[2048]{0:T(1024)}, u32[]{:S(2)}) copy-start(f32[2048]{0:T(1024)} %copy-done.41) | copy-start | bytes 24580
  1607.5 174.2 %copy-start.64 = (f32[16]{0:T(128)S(1)}, f32[16]{0:T(128)}, u32[]{:S(2)}) copy-start(f32[16]{0:T(128)} %get-tuple-element.129) | copy-start | bytes 196
  1789.4 123.6 %copy-start = (s32[8,1,6]{0,1,2:T(1,128)S(1)}, s32[8,1,6]{0,1,2:T(1,128)}, u32[]{:S(2)}) copy-start(s32[8,1,6]{0,1,2:T(1,128)} %param.22) | copy-start | bytes 580
  1914.5 78.3 %copy-start.60 = (s32[6]{0:T(128)}, s32[6]{0:T(128)S(1)}, u32[]{:S(2)}) copy-start(s32[6]{0:T(128)S(1)} %get-tuple-element.15) | copy-start | bytes 76
  2014.1 118.9 %copy-start.13 = (s32[8,1]{0,1:T(1,128)S(1)}, s32[8,1]{0,1:T(1,128)}, u32[]{:S(2)}) copy-start(s32[8,1]{0,1:T(1,128)} %param.23) | copy-start | bytes 100
  2014.1 120.2 %copy-start.58 = (pred[6]{0:T(512)(128)(4,1)S(1)}, pred[6]{0:T(512)(128)(4,1)}, u32[]{:S(2)}) copy-start(pred[6]{0:T(512)(128)(4,1)} %copy-done.57) | copy-start | bytes 22
  2015.0 121.2 %copy-start.52 = (pred[6]{0:T(512)(128)(4,1)S(1)}, pred[6]{0:T(512)(128)(4,1)}, u32[]{:S(2)}) copy-start(pred[6]{0:T(512)(128)(4,1)} %copy-done.51) | copy-start | bytes 22
  2015.0 124.8 %copy-start.55 = (pred[6]{0:T(512)(128)(4,1)S(1)}, pred[6]{0:T(512)(128)(4,1)}, u32[]{:S(2)}) copy-start(pred[6]{0:T(512)(128)(4,1)} %copy-done.54) | copy-start | bytes 22
  2015.0 126.6 %copy-start.53 = (pred[6]{0:T(512)(128)(4,1)S(1)}, pred[6]{0:T(512)(128)(4,1)}, u32[]{:S(2)}) copy-start(pred[6]{0:T(512)(128)(4,1)} %get-tuple-element.335) | copy-start | bytes 22
  2015.9 129.6 %copy-start.63 = (s32[6]{0:T(128)S(1)}, s32[6]{0:T(128)}, u32[]{:S(2)}) copy-start(s32[6]{0:T(128)} %get-tuple-element.19) | copy-start | bytes 76
  (47 other events, 372.9 us)
where the time goes:
time: 2260 us; the launch traced here: 2240 us
  blocking collectives  1970 us (87%)
  matrix products  106 us (5%)
  local copies, waits for them, and re-layouts  99.9 us (4%)
  other arithmetic  53 us (2%)
    unnamed x8, blocking collectives  519 us
    psum x8, blocking collectives, per_device(): lax.psum((jnp.sum(mismatch * mismatch), jnp.sum(variance + obs_err)), ('t...  515 us
    all_gather x8, blocking collectives, per_device(): lax.all_gather(delta_low, ('tile', 'lev'), axis=1, tiled=True)  423 us
    all_gather x8, blocking collectives, per_device(): lax.all_gather(anomaly_low, ('tile', 'lev'), axis=1, tiled=True)  416 us
    dot_general x8, matrix products, tile_update(): jnp.einsum('km,lmc->lkc', chosen_delta, gain_low, preferred_element_type=...  61.4 us
    all_gather x1, blocking collectives, per_device(): lax.all_gather(obs_height, ('tile', 'lev'), axis=1, tiled=True)  50.5 us
    all_gather x1, blocking collectives, per_device(): lax.all_gather(obs_place, ('tile', 'lev'), axis=1, tiled=True)  49.9 us

commit v1 on v0

v1 whole, which is shorter than its diff:
```python
import math

import jax
import jax.numpy as jnp
from jax import lax
from jax.experimental import pallas as pl
from jax.experimental.pallas import tpu as pltpu
from jax.sharding import PartitionSpec as P

MESH = pl.DeviceIdType.MESH
F32 = jnp.float32
BF16 = jnp.bfloat16

K = 80
NB = 8
B = 2048
OBLK = 128
NOB = 16
MAXB = 6
LEVD = 8
COLD = 512
GRP = 8
OWN = OBLK // GRP

EPS = 1e-05
INV_REACH = 4.0
INV_VREACH = 0.125
COUPLE = 4.0 / math.sqrt(B) / (K - 1)
SCOUPLE = 4.0 / math.sqrt(MAXB * OBLK) / (K - 1)


def device(x, y, core, z):
    return ((x * 4 + y) * 2 + core, z)


def kernel(
    state_hbm,
    prior_ref,
    value_ref,
    error_ref,
    place_ref,
    height_ref,
    blocks_ref,
    counts_ref,
    loc_hbm,
    mask_hbm,
    x_ref,
    post_ref,
    piece,
    yo,
    aux,
    pcol,
    mrow,
    maskv,
    ab,
    st,
    abc,
    stc,
    rows,
    dyb,
    dys,
    near,
    rr,
    aet,
    abt,
    dch,
    scl,
    locv,
    state_sem,
    loc_sem,
    mask_sem,
    psend,
    precv,
    ssend,
    srecv,
    bsend,
    brecv,
):
    t = lax.axis_index("tile")
    z = lax.axis_index("lev")
    x, y, core = t // 8, (t // 2) % 4, t % 2
    own = x * 4 + y
    seat = core * 4 + z

    load_state = pltpu.make_async_copy(state_hbm, x_ref, state_sem)
    load_state.start()
    load_mask = pltpu.make_async_copy(mask_hbm.at[:, own], maskv, mask_sem)
    load_mask.start()

    def load_loc(c):
        return pltpu.make_async_copy(loc_hbm.at[c], locv.at[c], loc_sem.at[c])

    for c in range(NB):
        load_loc(c).start()

    column = []
    for step in range(1, GRP):
        other = lax.rem(seat + step, GRP)
        column.append(device(x, y, other // 4, lax.rem(other, 4)))
    plane = []
    for dx in range(4):
        for dy in range(4):
            if dx or dy:
                plane.append(device(lax.rem(x + dx, 4), lax.rem(y + dy, 4), core, z))

    barrier = pltpu.get_barrier_semaphore()
    for peer in column + plane:
        pl.semaphore_signal(barrier, inc=1, device_id=peer, device_id_type=MESH)

    pad = jnp.zeros((16, 128 - 5 * OWN), F32)
    for e in range(NB):
        parts = [prior_ref[e, 16 * g : 16 * (g + 1), :] for g in range(5)]
        piece[seat, 1 + e] = jnp.concatenate(parts + [pad], axis=1)
    packed = jnp.concatenate(
        [value_ref[...], error_ref[...], place_ref[...] * INV_REACH, height_ref[...], jnp.zeros((NB, 64), F32)], axis=1
    )
    piece[seat, 0] = jnp.concatenate([packed, jnp.zeros((8, 128), F32)], axis=0)

    pl.semaphore_wait(barrier, len(column) + len(plane))

    def spread_pieces(part, first, count):
        for peer in column:
            ref = piece.at[seat, pl.ds(first, count)]
            pltpu.make_async_remote_copy(
                src_ref=ref,
                dst_ref=ref,
                send_sem=psend.at[part],
                recv_sem=precv.at[part],
                device_id=peer,
                device_id_type=MESH,
            ).start()

    def take_pieces(part, first, count, sem):
        ref = piece.at[pl.ds(0, GRP - 1), pl.ds(first, count)]
        pltpu.make_async_copy(ref, ref, sem.at[part]).wait()

    spread_pieces(0, 0, 2)
    spread_pieces(1, 2, NB - 1)

    load_mask.wait()
    eye = lax.broadcasted_iota(jnp.int32, (NOB, NOB), 0) == lax.broadcasted_iota(jnp.int32, (NOB, NOB), 1)
    for e in range(1, NB):
        for c in range(e):
            chosen = jnp.where(eye, maskv[e, c : c + 1, :].astype(F32), 0.0)
            mrow[e, c] = jnp.broadcast_to(jnp.sum(chosen, axis=1, keepdims=True), (NOB, 128))

    group = lax.broadcasted_iota(jnp.int32, (16, 128), 1) // OWN

    def gathered(slab, g):
        total = jnp.zeros((16, 128), F32)
        for s in range(GRP):
            moved = pltpu.roll(piece[s, slab], ((s - g) * OWN) % 128, 1)
            total = jnp.where(group == s, moved, total)
        return total

    def unpack(e):
        for g in range(5):
            yo[e, pl.ds(16 * g, 16), :] = gathered(1 + e, g)

    take_pieces(0, 0, 2, precv)
    for g in range(4):
        aux[g] = gathered(0, g)[0:NB]
    unpack(0)

    def copies(e, ref, send, recv):
        mine = ref.at[e, own]
        for peer in plane:
            pltpu.make_async_remote_copy(
                src_ref=mine,
                dst_ref=mine,
                send_sem=send.at[e],
                recv_sem=recv.at[e],
                device_id=peer,
                device_id_type=MESH,
            ).start()

    def publish(e):
        now = yo[e]
        average = jnp.sum(now, axis=0, keepdims=True) * (1.0 / K)
        anomaly = now - average
        variance = jnp.sum(anomaly * anomaly, axis=0, keepdims=True) * (1.0 / (K - 1)) + EPS
        here = pl.ds(e, 1)
        st[e, own] = jnp.concatenate(
            [
                variance,
                aux[0, here, :] - average,
                aux[1, here, :],
                aux[2, here, :],
                aux[3, here, :],
                jnp.zeros((3, 128), F32),
            ],
            axis=0,
        )
        copies(e, st, ssend, srecv)
        ab[e, own] = anomaly.astype(BF16)
        copies(e, ab, bsend, brecv)

    def take(e, ref, sem):
        some = ref.at[e, pl.ds(0, NOB - 1)]
        pltpu.make_async_copy(some, some, sem.at[e]).wait()

    publish(0)
    take_pieces(1, 2, NB - 1, precv)
    pl.loop(1, NB)(unpack)

    @pl.loop(0, NB)
    def _(e):
        pcol[e] = jnp.transpose(jnp.broadcast_to(aux[2, pl.ds(e, 1), :], (128, 128)))

    def nearness(c, e):
        mine = pcol[e]
        for b in range(NOB):
            cut = slice(b * 128, (b + 1) * 128)
            gap = mine - st[c, b, 3:4, :]
            near[:, cut] = (mrow[e, c, b : b + 1, :] * pl.reciprocal(1.0 + gap * gap, approx=True)).astype(BF16)

    def transposed(e):
        now = yo[e]
        average = jnp.sum(now, axis=0, keepdims=True) * (1.0 / K)
        aet[...] = jnp.transpose(now - average).astype(BF16)

    def regress(c, e):
        for part in range(4):
            cut = slice(part * 512, (part + 1) * 512)
            theirs = jnp.concatenate([ab[c, part * 4 + i] for i in range(4)], axis=1)
            covar = jnp.dot(aet[...], theirs, preferred_element_type=F32)
            rr[:, cut] = covar.astype(BF16) * near[:, cut]
        yo[e] += lax.dot_general(dys[...], rr[...], (((1,), (1,)), ((), ())), preferred_element_type=F32)

    level = (lax.broadcasted_iota(jnp.int32, (LEVD, 128), 0) + z * LEVD).astype(F32) + 0.5

    load_state.wait()

    @pl.loop(0, NB)
    def _(c):
        @pl.when(c < NB - 1)
        def _():
            transposed(c + 1)

        take(c, st, srecv)
        variance, miss, error = st[c, :, 0, :], st[c, :, 1, :], st[c, :, 2, :]
        gamma = jnp.sum(miss * miss, keepdims=True) / jnp.sum(variance + error, keepdims=True)
        inflated = gamma * variance
        both = inflated + error
        rows[0] = inflated / both * miss
        rows[1] = jnp.sqrt(gamma * error / both) - 1.0
        rows[2] = COUPLE / variance

        @pl.when(c < NB - 1)
        def _():
            nearness(c, c + 1)

        take(c, ab, brecv)
        for b in range(NOB):
            low = (rows[0, b : b + 1, :] + rows[1, b : b + 1, :] * ab[c, b].astype(F32)).astype(BF16)
            dyb[b] = low
            dys[:, b * 128 : (b + 1) * 128] = (low.astype(F32) * rows[2, b : b + 1, :]).astype(BF16)

        @pl.when(c < NB - 1)
        def _():
            regress(c, c + 1)
            publish(c + 1)

        yo[c] += dyb[own].astype(F32)

        @pl.loop(c + 2, NB)
        def _(e):
            transposed(e)
            nearness(c, e)
            regress(c, e)

        abc[...] = ab[c]
        stc[...] = st[c]
        load_loc(c).wait()
        used = counts_ref[c, 0]
        for i in range(MAXB):
            block = blocks_ref[c, 0, i]
            cut = slice(i * 128, (i + 1) * 128)
            abt[cut, :] = jnp.transpose(abc[block].astype(F32)).astype(BF16)
            dch[:, cut] = dyb[block]
            theirs = stc[block]
            gap = (level - theirs[4:5, :]) * INV_VREACH
            weight = jnp.where(i < used, SCOUPLE, 0.0) / theirs[0:1, :]
            scl[:, i, :] = weight / (1.0 + gap * gap)

        def one_level(l):
            block = x_ref[l]
            low = (block - jnp.sum(block, axis=0, keepdims=True) * (1.0 / K)).astype(BF16)
            covar = jnp.dot(abt[...], low, preferred_element_type=F32)
            gain = covar.astype(BF16) * locv[c]
            delta = jnp.concatenate(
                [
                    (dch[:, i * 128 : (i + 1) * 128].astype(F32) * scl[l, i : i + 1, :]).astype(BF16)
                    for i in range(MAXB)
                ],
                axis=1,
            )
            x_ref[l] = block + jnp.dot(delta, gain, preferred_element_type=F32)

        pl.loop(0, LEVD, unroll=2)(one_level)

    for e in range(NB):
        post_ref[e] = pltpu.roll(yo[e], lax.rem(128 - seat * OWN, 128), 1)[:, 0:OWN]

    take_pieces(0, 0, 2, psend)
    take_pieces(1, 2, NB - 1, psend)

    @pl.loop(0, NB)
    def _(c):
        take(c, st, ssend)
        take(c, ab, bsend)


def per_device(*args):
    vmem = pl.BlockSpec(memory_space=pltpu.VMEM)
    smem = pl.BlockSpec(memory_space=pltpu.SMEM)
    hbm = pl.BlockSpec(memory_space=pl.ANY)
    dma = pltpu.SemaphoreType.DMA
    return pl.pallas_call(
        kernel,
        out_shape=(
            jax.ShapeDtypeStruct((LEVD, K, COLD), F32),
            jax.ShapeDtypeStruct((NB, K, OWN), F32),
        ),
        in_specs=[hbm, vmem, vmem, vmem, vmem, vmem, smem, smem, hbm, hbm],
        out_specs=(vmem, vmem),
        scratch_shapes=[
            pltpu.VMEM((GRP, 1 + NB, 16, 128), F32),
            pltpu.VMEM((NB, K, 128), F32),
            pltpu.VMEM((4, NB, 128), F32),
            pltpu.VMEM((NB, 128, 128), F32),
            pltpu.VMEM((NB, NB, NOB, 128), F32),
            pltpu.VMEM((NB, NB, NOB), jnp.int32),
            pltpu.VMEM((NB, NOB, K, 128), BF16),
            pltpu.VMEM((NB, NOB, 8, 128), F32),
            pltpu.VMEM((NOB, K, 128), BF16),
            pltpu.VMEM((NOB, 8, 128), F32),
            pltpu.VMEM((3, NOB, 128), F32),
            pltpu.VMEM((NOB, K, 128), BF16),
            pltpu.VMEM((K, B), BF16),
            pltpu.VMEM((128, B), BF16),
            pltpu.VMEM((128, B), BF16),
            pltpu.VMEM((128, K), BF16),
            pltpu.VMEM((MAXB * 128, K), BF16),
            pltpu.VMEM((K, MAXB * 128), BF16),
            pltpu.VMEM((LEVD, 8, 128), F32),
            pltpu.VMEM((NB, MAXB * 128, COLD), BF16),
            dma(()),
            dma((NB,)),
            dma(()),
            dma((2,)),
            dma((2,)),
            dma((NB,)),
            dma((NB,)),
            dma((NB,)),
            dma((NB,)),
        ],
        compiler_params=pltpu.CompilerParams(
            collective_id=0, has_side_effects=True, vmem_limit_bytes=48 * 2**20
        ),
    )(*args)


def solution(mesh):
    placed = (
        P("lev", None, "tile"),
        P(None, None, ("tile", "lev")),
        P(None, ("tile", "lev")),
        P(None, ("tile", "lev")),
        P(None, ("tile", "lev")),
        P(None, ("tile", "lev")),
        P(None, "tile", None),
        P(None, "tile"),
        P(None, None, "tile"),
        P(),
    )
    return jax.shard_map(
        per_device,
        mesh=mesh,
        in_specs=placed,
        out_specs=(P("lev", None, "tile"), P(None, None, ("tile", "lev"))),
        check_vma=False,
    )
```

time: 2260 us -> 92 us (0.04)
  blocking collectives: 1970 us -> 0 us
  matrix products: 106 us -> 0 us
  local copies, waits for them, and re-layouts: 99.9 us -> 9.38 us
  Pallas kernels: 0 us -> 81.5 us
  other arithmetic: 53 us -> 0 us
    all_gather x18 -> x0, blocking collectives: 940 us -> none  [the longest x8 423 us: per_device(): lax.all_gather(delta_low, ('tile', 'lev'), axis=1, tiled=True)]
    unnamed x8 -> x0, blocking collectives: 519 us -> none
    psum x8 -> x0, blocking collectives: 515 us -> none  [per_device(): lax.psum((jnp.sum(mismatch * mismatch), jnp.sum(variance + obs_err)), ('t...]
    dot_general x36 -> x0, matrix products: 106 us -> none  [the longest x8 61.4 us: tile_update(): jnp.einsum('km,lmc->lkc', chosen_delta, gain_low, preferred_element_type=...]
    pallas_call x0 -> x1, Pallas kernels: none -> 81.5 us  [per_device(): pl.pallas_call(kernel, out_shape=(jax.ShapeDtypeStruct((LEVD, K, COLD), F...]
    gather x60 -> x0, local copies, waits for them, and re-layouts: 40.2 us -> none  [the longest x32 24.5 us: pick_blocks(): chosen = jnp.take(shaped, block_ids, axis=values.ndim - 1)]
    reshape x32 -> x0, local copies, waits for them, and re-layouts: 24.9 us -> none  [the longest x16 14 us: pick_blocks(): shaped = values.reshape(values.shape[:-1] + (NOB, OBLK))]
where the time goes in v1:
time: 92 us; the launch traced here: 91.6 us
  Pallas kernels  81.5 us (89%)
  local copies, waits for them, and re-layouts  9.38 us (10%)
    pallas_call x1, Pallas kernels, per_device(): pl.pallas_call(kernel, out_shape=(jax.ShapeDtypeStruct((LEVD, K, COLD), F...  81.5 us
    unnamed x16, local copies, waits for them, and re-layouts  8.62 us

profile of v1, /device:TPU:0, one launch (start us, length us, event | category | flops | bytes accessed | tf_op | source)
XLA Modules:
  0.0 91.6 jit_solution(12833091103730363949)
XLA Ops:
  0.6 0.8 copy.13.blocks_ref
  1.4 0.7 copy.14.counts_ref
  2.1 1.0 %copy.12.prior_ref = f32[8,80,16]{2,1,0:T(8,128)S(1)} copy(f32[8,80,16]{1,2,0:T(8,128)} %param.11) | data formatting | bytes 81920 | tf_op args[1]
  3.1 0.0 copy-start
  3.1 1.3 %copy-done = f32[8,80,512]{2,1,0:T(8,128)S(1)} copy-done((f32[8,80,512]{2,1,0:T(8,128)S(1)}, f32[8,80,512]{2,1,0:T(8,128)}, u32[]{:S(2)}) %copy-start) | copy-done | bytes 1310744
  4.4 0.0 copy-start.1
  4.4 1.0 %copy-done.1 = s32[8,16,8,16]{3,2,1,0:T(8,128)S(1)} copy-done((s32[8,16,8,16]{3,2,1,0:T(8,128)S(1)}, s32[8,16,8,16]{3,2,1,0:T(8,128)}, u32[]{:S(2)}) %copy-start.1) | copy-done | bytes 65560
  5.5 0.0 copy-start.2
  5.5 0.7 copy-done.2
  6.2 0.0 copy-start.3
  6.2 0.7 copy-done.3
  6.8 0.0 copy-start.4
  6.8 0.7 copy-done.4
  7.5 0.0 copy-start.5
  7.5 0.7 copy-done.5
  8.2 81.5 %shard_map.113 = (f32[8,80,512]{2,1,0:T(8,128)S(1)}, f32[8,80,16]{2,1,0:T(8,128)S(1)}) custom-call(f32[8,80,512]{2,1,0:T(8,128)S(1)} %copy-done, f32[8,80,16]{2,1,0:T(8,128)S(1)} %copy.12.prior_ref, f32[8,16]{1,0:T(8,128)S(1)} %copy-done.2, f32[8,16]{1,0:T(8,128)S(1)} %copy-done.3, f32[8,16]{1,0:T(8,128)S(1)} %copy-done.4, f32[8,16]{1,0:T(8,128)S(1)} %copy-done.5, ...), custom_call_target="tpu_custom_call" | custom-call | tf_op jit(solution)/shard_map/pallas_call | solution.py:319
  89.8 0.8 copy.15
  90.5 1.1 %copy.17 = f32[8,80,512]{2,1,0:T(8,128)} copy(f32[8,80,512]{2,1,0:T(8,128)S(1)} %get-tuple-element.6) | data formatting | bytes 2621440
Async XLA Ops:
  3.1 1.3 %copy-start = (f32[8,80,512]{2,1,0:T(8,128)S(1)}, f32[8,80,512]{2,1,0:T(8,128)}, u32[]{:S(2)}) copy-start(f32[8,80,512]{2,1,0:T(8,128)} %state_hbm.1) | copy-start | bytes 3932164
  4.4 1.0 %copy-start.1 = (s32[8,16,8,16]{3,2,1,0:T(8,128)S(1)}, s32[8,16,8,16]{3,2,1,0:T(8,128)}, u32[]{:S(2)}) copy-start(s32[8,16,8,16]{3,2,1,0:T(8,128)} %mask_hbm.1) | copy-start | bytes 196612
  5.5 0.7 copy-start.2
  6.2 0.7 copy-start.3
  6.8 0.7 copy-start.4
  7.5 0.7 copy-start.5

commit v2 on v1

v2 whole, which is shorter than its diff:
```python
import math

import jax
import jax.numpy as jnp
from jax import lax
from jax.experimental import pallas as pl
from jax.experimental.pallas import tpu as pltpu
from jax.sharding import PartitionSpec as P

MESH = pl.DeviceIdType.MESH
F32 = jnp.float32
BF16 = jnp.bfloat16

K = 80
NB = 8
B = 2048
OBLK = 128
NOB = 16
MAXB = 6
LEVD = 8
COLD = 512
QUAD = 4
GRP = 8
OWN = OBLK // GRP

EPS = 1e-05
INV_REACH = 4.0
INV_VREACH = 0.125
COUPLE = 4.0 / math.sqrt(B) / (K - 1)
SCOUPLE = 4.0 / math.sqrt(MAXB * OBLK) / (K - 1)


def device(x, y, core, z):
    return ((x * 4 + y) * 2 + core, z)


def kernel(
    state_hbm,
    prior_hbm,
    value_hbm,
    error_hbm,
    place_hbm,
    height_hbm,
    blocks_hbm,
    counts_hbm,
    loc_hbm,
    mask_hbm,
    x_ref,
    post_ref,
    prior,
    vectors,
    blocks_ref,
    counts_ref,
    piece,
    yo,
    yx,
    yt,
    aux,
    pcol,
    mrow,
    maskv,
    ab,
    st,
    hx,
    abc,
    vhc,
    rows,
    dyb,
    dys,
    near,
    rr,
    aet,
    abt,
    dch,
    scl,
    locv,
    in_sem,
    loc_sem,
    psend,
    precv,
    hsend,
    hrecv,
    ssend,
    srecv,
    bsend,
    brecv,
    ysend,
    yrecv,
):
    t = lax.axis_index("tile")
    z = lax.axis_index("lev")
    x, y, core = t // 8, (t // 2) % 4, t % 2
    own = x * 4 + y
    seat = core * 4 + z
    sibling = device(x, y, 1 - core, z)

    column = []
    for step in (4, 2, 6, 1, 3, 5, 7):
        other = lax.rem(seat + step, GRP)
        column.append(device(x, y, other // 4, lax.rem(other, 4)))
    hops = [(min(dx, 4 - dx) + min(dy, 4 - dy), dx, dy) for dx in range(4) for dy in range(4) if dx or dy]
    plane = []
    for _, dx, dy in sorted(hops, key=lambda hop: -hop[0]):
        plane.append(device(lax.rem(x + dx, 4), lax.rem(y + dy, 4), core, z))

    barrier = pltpu.get_barrier_semaphore()
    for peer in plane + column:
        pl.semaphore_signal(barrier, inc=1, device_id=peer, device_id_type=MESH)

    small = [
        pltpu.make_async_copy(src, dst, in_sem.at[i])
        for i, (src, dst) in enumerate(
            [
                (prior_hbm, prior),
                (value_hbm, vectors.at[0]),
                (error_hbm, vectors.at[1]),
                (place_hbm, vectors.at[2]),
                (height_hbm, vectors.at[3]),
                (mask_hbm.at[:, own], maskv),
                (blocks_hbm, blocks_ref),
                (counts_hbm, counts_ref),
                (state_hbm, x_ref),
            ]
        )
    ]
    for copy in small:
        copy.start()

    def load_loc(c):
        return pltpu.make_async_copy(loc_hbm.at[c], locv.at[c], loc_sem.at[c])

    for c in range(NB):
        load_loc(c).start()

    for copy in small[:5]:
        copy.wait()
    for e in range(NB):
        piece[seat, 1 + e] = jnp.concatenate([prior[e], jnp.zeros((OWN, 128 - K), F32)], axis=1)
    square = jnp.concatenate([vectors[g] for g in range(4)] + [jnp.zeros((128 - 4 * NB, OWN), F32)], axis=0)
    square = jnp.concatenate([square, jnp.zeros((128, 128 - OWN), F32)], axis=1)
    piece[seat, 0] = jnp.transpose(square)[0:OWN]

    pl.semaphore_wait(barrier, len(column) + len(plane))

    def send(ref, send_sem, recv_sem, peers):
        for peer in peers:
            pltpu.make_async_remote_copy(
                src_ref=ref,
                dst_ref=ref,
                send_sem=send_sem,
                recv_sem=recv_sem,
                device_id=peer,
                device_id_type=MESH,
            ).start()

    def settle(ref, sem):
        pltpu.make_async_copy(ref, ref, sem).wait()

    send(piece.at[seat, pl.ds(0, 2)], psend.at[0], precv.at[0], column)
    send(piece.at[seat, pl.ds(2, NB - 1)], psend.at[1], precv.at[1], column)
    early = piece.at[pl.ds(0, GRP - 1), pl.ds(0, 2)]
    late = piece.at[pl.ds(0, GRP - 1), pl.ds(2, NB - 1)]

    small[5].wait()
    eye = lax.broadcasted_iota(jnp.int32, (NOB, NOB), 0) == lax.broadcasted_iota(jnp.int32, (NOB, NOB), 1)
    for e in range(1, NB):
        for c in range(e):
            chosen = jnp.where(eye, maskv[e, c : c + 1, :].astype(F32), 0.0)
            mrow[e, c] = jnp.broadcast_to(jnp.sum(chosen, axis=1, keepdims=True), (NOB, 128))

    def unpack(e):
        yo[e] = jnp.transpose(piece[:, 1 + e].reshape(128, 128))[0:K]

    settle(early, precv.at[0])
    vector_rows = jnp.transpose(piece[:, 0].reshape(128, 128))
    for g in range(4):
        aux[g] = vector_rows[g * NB : (g + 1) * NB] * (INV_REACH if g == 2 else 1.0)
    unpack(0)
    for e in range(NB):
        for g in range(1, 4):
            hx[own, e, g - 1 : g, :] = aux[g, e : e + 1, :]
        hx[own, e, 3:4, :] = jnp.zeros((1, 128), F32)

    def publish(e):
        now = yo[e]
        average = jnp.sum(now, axis=0, keepdims=True) * (1.0 / K)
        anomaly = now - average
        variance = jnp.sum(anomaly * anomaly, axis=0, keepdims=True) * (1.0 / (K - 1)) + EPS
        st[e, own, 0:1, :] = variance
        st[e, own, 1:2, :] = aux[0, pl.ds(e, 1), :] - average
        send(st.at[e, own], ssend.at[e], srecv.at[e], plane)
        ab[e, own] = anomaly.astype(BF16)
        send(ab.at[e, own], bsend.at[e], brecv.at[e], plane)

    def take(e, ref, sem):
        settle(ref.at[e, pl.ds(0, NOB - 1)], sem.at[e])

    send(hx.at[own, 0], hsend.at[0], hrecv.at[0], plane)
    publish(0)
    send(hx.at[own, pl.ds(1, NB - 1)], hsend.at[1], hrecv.at[1], plane)
    hx_first = hx.at[pl.ds(0, NOB - 1), 0]
    hx_rest = hx.at[pl.ds(0, NOB - 1), pl.ds(1, NB - 1)]
    settle(late, precv.at[1])
    pl.loop(1, NB)(unpack)

    @pl.loop(0, NB)
    def _(e):
        pcol[e] = jnp.transpose(jnp.broadcast_to(aux[2, pl.ds(e, 1), :], (128, 128)))

    def nearness(c, e):
        mine = pcol[e]
        for b in range(NOB):
            cut = slice(b * 128, (b + 1) * 128)
            gap = mine - hx[b, c, 1:2, :]
            near[:, cut] = pl.reciprocal(1.0 + gap * gap, approx=True).astype(BF16)

    def transposed(e):
        now = yo[e]
        average = jnp.sum(now, axis=0, keepdims=True) * (1.0 / K)
        aet[...] = jnp.transpose(now - average).astype(BF16)

    def regress(c, e):
        for part in range(4):
            cut = slice(part * 512, (part + 1) * 512)
            theirs = jnp.concatenate(
                [ab[c, b] * mrow[e, c, b : b + 1, :].astype(BF16) for b in range(part * 4, part * 4 + 4)], axis=1
            )
            covar = jnp.dot(aet[...], theirs, preferred_element_type=F32)
            rr[:, cut] = covar.astype(BF16) * near[:, cut]
        yo[e] += lax.dot_general(dys[...], rr[...], (((1,), (1,)), ((), ())), preferred_element_type=F32)

    level = (lax.broadcasted_iota(jnp.int32, (LEVD, 128), 0) + z * LEVD).astype(F32) + 0.5

    for copy in small[6:]:
        copy.wait()
    settle(hx_first, hrecv.at[0])

    def hand_over(e):
        return pltpu.make_async_remote_copy(
            src_ref=yo.at[e],
            dst_ref=yx.at[e],
            send_sem=ysend.at[e],
            recv_sem=yrecv.at[e],
            device_id=sibling,
            device_id_type=MESH,
        )

    def one_level(unit):
        c, l = unit // LEVD, unit % LEVD
        block = x_ref[l]
        low = (block - jnp.sum(block, axis=0, keepdims=True) * (1.0 / K)).astype(BF16)
        covar = jnp.dot(abt[c], low, preferred_element_type=F32)
        gain = covar.astype(BF16) * locv[c]
        delta = jnp.concatenate(
            [
                (dch[c, :, i * 128 : (i + 1) * 128].astype(F32) * scl[c, l, i : i + 1, :]).astype(BF16)
                for i in range(MAXB)
            ],
            axis=1,
        )
        x_ref[l] = block + jnp.dot(delta, gain, preferred_element_type=F32)

    def state_quad(quad):
        for i in range(QUAD):
            one_level(quad * QUAD + i)

    @pl.loop(0, NB)
    def _(c):
        @pl.when(c == 1)
        def _():
            settle(hx_rest, hrecv.at[1])

        @pl.when((c >= 1) & (c < NB - 1))
        def _():
            @pl.when(core == (c + 1) % 2)
            def _():
                hand_over(c + 1).wait_send()

            @pl.when(core != (c + 1) % 2)
            def _():
                hand_over(c + 1).wait_recv()
                yo[c + 1] = yx[c + 1]

        @pl.when(c < NB - 1)
        def _():
            transposed(c + 1)
            nearness(c, c + 1)

        take(c, st, srecv)
        variance, miss, error = st[c, :, 0, :], st[c, :, 1, :], hx[:, c, 0, :]
        gamma = jnp.sum(miss * miss, keepdims=True) / jnp.sum(variance + error, keepdims=True)
        inflated = gamma * variance
        both = inflated + error
        rows[0] = inflated / both * miss
        rows[1] = jnp.sqrt(gamma * error / both) - 1.0
        rows[2] = COUPLE / variance

        take(c, ab, brecv)
        for b in range(NOB):
            low = (rows[0, b : b + 1, :] + rows[1, b : b + 1, :] * ab[c, b].astype(F32)).astype(BF16)
            dyb[b] = low
            dys[:, b * 128 : (b + 1) * 128] = (low.astype(F32) * rows[2, b : b + 1, :]).astype(BF16)

        @pl.when(c < NB - 1)
        def _():
            regress(c, c + 1)
            publish(c + 1)

        @pl.loop(c + 2 + (c + core) % 2, NB, step=2)
        def _(e):
            transposed(e)
            nearness(c, e)
            regress(c, e)

            @pl.when(e == c + 2)
            def _():
                hand_over(e).start()

        abc[...] = ab[c]
        vhc[:, 0, :] = variance
        vhc[:, 1, :] = hx[:, c, 2, :]
        load_loc(c).wait()
        used = counts_ref[0, c]
        for i in range(MAXB):
            block = blocks_ref[i, 0, c]
            cut = slice(i * 128, (i + 1) * 128)
            abt[c, cut, :] = jnp.transpose(abc[block].astype(F32)).astype(BF16)
            dch[c, :, cut] = dyb[block]
            theirs = vhc[block]
            gap = (level - theirs[1:2, :]) * INV_VREACH
            weight = jnp.where(i < used, SCOUPLE, 0.0) / theirs[0:1, :]
            scl[c, :, i, :] = weight / (1.0 + gap * gap)

        first = jnp.where(c == 0, 0, 2 * c - 1)
        last = jnp.where(c >= NB - 2, 2 * c + 2, 2 * c + 1)
        pl.loop(jnp.where(c == NB - 1, 2 * c, first), last)(state_quad)

        final = yo[c] + dyb[own].astype(F32)
        yt[...] = jnp.transpose(final)
        post_ref[c] = yt[pl.ds(pl.multiple_of(seat * OWN, OWN), OWN), :]

    settle(early, psend.at[0])
    settle(late, psend.at[1])
    settle(hx_first, hsend.at[0])
    settle(hx_rest, hsend.at[1])

    @pl.loop(0, NB)
    def _(c):
        take(c, st, ssend)
        take(c, ab, bsend)


def per_device(state, prior, value, error, place, height, blocks, counts, loc, mask):
    vmem = pl.BlockSpec(memory_space=pltpu.VMEM)
    hbm = pl.BlockSpec(memory_space=pltpu.HBM)
    dma = pltpu.SemaphoreType.DMA
    analysis, post = pl.pallas_call(
        kernel,
        out_shape=(
            jax.ShapeDtypeStruct((LEVD, K, COLD), F32),
            jax.ShapeDtypeStruct((NB, OWN, K), F32),
        ),
        in_specs=[hbm] * 10,
        out_specs=(vmem, vmem),
        scratch_shapes=[
            pltpu.VMEM((NB, OWN, K), F32),
            pltpu.VMEM((4, NB, OWN), F32),
            pltpu.SMEM((MAXB, 1, NB), jnp.int32),
            pltpu.SMEM((1, NB), jnp.int32),
            pltpu.VMEM((GRP, 1 + NB, OWN, 128), F32),
            pltpu.VMEM((NB, K, 128), F32),
            pltpu.VMEM((NB, K, 128), F32),
            pltpu.VMEM((128, K), F32),
            pltpu.VMEM((4, NB, 128), F32),
            pltpu.VMEM((NB, 128, 128), F32),
            pltpu.VMEM((NB, NB, NOB, 128), F32),
            pltpu.VMEM((NB, NB, NOB), jnp.int32),
            pltpu.VMEM((NB, NOB, K, 128), BF16),
            pltpu.VMEM((NB, NOB, 2, 128), F32),
            pltpu.VMEM((NOB, NB, 4, 128), F32),
            pltpu.VMEM((NOB, K, 128), BF16),
            pltpu.VMEM((NOB, 2, 128), F32),
            pltpu.VMEM((3, NOB, 128), F32),
            pltpu.VMEM((NOB, K, 128), BF16),
            pltpu.VMEM((K, B), BF16),
            pltpu.VMEM((128, B), BF16),
            pltpu.VMEM((128, B), BF16),
            pltpu.VMEM((128, K), BF16),
            pltpu.VMEM((NB, MAXB * 128, K), BF16),
            pltpu.VMEM((NB, K, MAXB * 128), BF16),
            pltpu.VMEM((NB, LEVD, 8, 128), F32),
            pltpu.VMEM((NB, MAXB * 128, COLD), BF16),
            dma((9,)),
            dma((NB,)),
            dma((2,)),
            dma((2,)),
            dma((2,)),
            dma((2,)),
            dma((NB,)),
            dma((NB,)),
            dma((NB,)),
            dma((NB,)),
            dma((NB,)),
            dma((NB,)),
        ],
        compiler_params=pltpu.CompilerParams(
            collective_id=0, has_side_effects=True, vmem_limit_bytes=48 * 2**20
        ),
    )(
        *(
            pltpu.with_memory_space_constraint(array, pltpu.HBM)
            for array in (
                state,
                jnp.swapaxes(prior, 1, 2),
                value,
                error,
                place,
                height,
                jnp.transpose(blocks, (2, 1, 0)),
                jnp.transpose(counts),
                loc,
                mask,
            )
        )
    )
    return analysis, jnp.swapaxes(post, 1, 2)


def solution(mesh):
    placed = (
        P("lev", None, "tile"),
        P(None, None, ("tile", "lev")),
        P(None, ("tile", "lev")),
        P(None, ("tile", "lev")),
        P(None, ("tile", "lev")),
        P(None, ("tile", "lev")),
        P(None, "tile", None),
        P(None, "tile"),
        P(None, None, "tile"),
        P(),
    )
    return jax.shard_map(
        per_device,
        mesh=mesh,
        in_specs=placed,
        out_specs=(P("lev", None, "tile"), P(None, None, ("tile", "lev"))),
        check_vma=False,
    )
```

time: 92 us -> 76.9 us (0.84)
  local copies, waits for them, and re-layouts: 9.38 us -> 1.69 us
  Pallas kernels: 81.5 us -> 74.5 us
    pallas_call x1, Pallas kernels: 81.5 us -> 74.5 us  [per_device(): pl.pallas_call(kernel, out_shape=(jax.ShapeDtypeStruct((LEVD, K, COLD), F...]
    unnamed x16 -> x2, local copies, waits for them, and re-layouts: 8.62 us -> 1.69 us
where the time goes in v2:
time: 76.9 us; the launch traced here: 76.8 us
  Pallas kernels  74.5 us (97%)
  local copies, waits for them, and re-layouts  1.69 us (2%)
    pallas_call x1, Pallas kernels, per_device(): pl.pallas_call(kernel, out_shape=(jax.ShapeDtypeStruct((LEVD, K, COLD), F...  74.5 us
    unnamed x2, local copies, waits for them, and re-layouts  1.69 us

profile of v2, /device:TPU:0, one launch (start us, length us, event | category | flops | bytes accessed | tf_op | source)
XLA Modules:
  0.0 76.8 jit_solution(15802647071725579722)
XLA Ops:
  0.6 74.5 %shard_map.113 = (f32[8,80,512]{2,1,0:T(8,128)S(1)}, f32[8,16,80]{2,1,0:T(8,128)S(1)}) custom-call(f32[8,80,512]{2,1,0:T(8,128)} %state_hbm.1, f32[8,16,80]{2,1,0:T(8,128)} %bitcast.5, f32[8,16]{1,0:T(8,128)} %value_hbm.1, f32[8,16]{1,0:T(8,128)} %error_hbm.1, f32[8,16]{1,0:T(8,128)} %place_hbm.1, f32[8,16]{1,0:T(8,128)} %height_hbm.1, s32[6,1,8]{2,1,0:T(1,128)} %bitcast.6, ...), custom_call_target="tpu_custom_call" | custom-call | tf_op jit(solution)/shard_map/pallas_call | solution.py:357
  75.1 1.1 %copy.14 = f32[8,80,512]{2,1,0:T(8,128)} copy(f32[8,80,512]{2,1,0:T(8,128)S(1)} %get-tuple-element.8) | data formatting | bytes 2621440
  76.2 0.6 copy.15

commit v3 on v2

--- a/solution.py
+++ b/solution.py
@@ -51,6 +51,7 @@
     vectors,
     blocks_ref,
     counts_ref,
+    mine,
     piece,
     yo,
     yx,
@@ -92,7 +93,6 @@
     x, y, core = t // 8, (t // 2) % 4, t % 2
     own = x * 4 + y
     seat = core * 4 + z
-    sibling = device(x, y, 1 - core, z)
 
     column = []
     for step in (4, 2, 6, 1, 3, 5, 7):
@@ -134,19 +134,25 @@
 
     for copy in small[:5]:
         copy.wait()
-    for e in range(NB):
-        piece[seat, 1 + e] = jnp.concatenate([prior[e], jnp.zeros((OWN, 128 - K), F32)], axis=1)
     square = jnp.concatenate([vectors[g] for g in range(4)] + [jnp.zeros((128 - 4 * NB, OWN), F32)], axis=0)
     square = jnp.concatenate([square, jnp.zeros((128, 128 - OWN), F32)], axis=1)
-    piece[seat, 0] = jnp.transpose(square)[0:OWN]
+    behind = jnp.transpose(square)[0:OWN, 0 : 128 - K]
+    for e in range(NB):
+        mine[e] = jnp.concatenate([prior[e], behind if e == 0 else jnp.zeros((OWN, 128 - K), F32)], axis=1)
+    piece[seat, 0] = mine[0]
+    piece[seat, 1] = mine[1]
+
+    @pl.when(seat >= 2)
+    def _():
+        piece[seat, 2] = mine[seat]
 
     pl.semaphore_wait(barrier, len(column) + len(plane))
 
-    def send(ref, send_sem, recv_sem, peers):
+    def send(ref, send_sem, recv_sem, peers, target=None):
         for peer in peers:
             pltpu.make_async_remote_copy(
                 src_ref=ref,
-                dst_ref=ref,
+                dst_ref=ref if target is None else target,
                 send_sem=send_sem,
                 recv_sem=recv_sem,
                 device_id=peer,
@@ -156,10 +162,7 @@
     def settle(ref, sem):
         pltpu.make_async_copy(ref, ref, sem).wait()
 
-    send(piece.at[seat, pl.ds(0, 2)], psend.at[0], precv.at[0], column)
-    send(piece.at[seat, pl.ds(2, NB - 1)], psend.at[1], precv.at[1], column)
-    early = piece.at[pl.ds(0, GRP - 1), pl.ds(0, 2)]
-    late = piece.at[pl.ds(0, GRP - 1), pl.ds(2, NB - 1)]
+    send(mine.at[0], psend.at[0], precv.at[0], column, piece.at[seat, 0])
 
     small[5].wait()
     eye = lax.broadcasted_iota(jnp.int32, (NOB, NOB), 0) == lax.broadcasted_iota(jnp.int32, (NOB, NOB), 1)
@@ -168,14 +171,14 @@
             chosen = jnp.where(eye, maskv[e, c : c + 1, :].astype(F32), 0.0)
             mrow[e, c] = jnp.broadcast_to(jnp.sum(chosen, axis=1, keepdims=True), (NOB, 128))
 
-    def unpack(e):
-        yo[e] = jnp.transpose(piece[:, 1 + e].reshape(128, 128))[0:K]
-
-    settle(early, precv.at[0])
-    vector_rows = jnp.transpose(piece[:, 0].reshape(128, 128))
+    def unpack(slot):
+        return jnp.transpose(piece[:, slot].reshape(128, 128))
+
+    settle(piece.at[pl.ds(0, GRP - 1), 0], precv.at[0])
+    first = unpack(0)
+    yo[0] = first[0:K]
     for g in range(4):
-        aux[g] = vector_rows[g * NB : (g + 1) * NB] * (INV_REACH if g == 2 else 1.0)
-    unpack(0)
+        aux[g] = first[K + g * NB : K + (g + 1) * NB] * (INV_REACH if g == 2 else 1.0)
     for e in range(NB):
         for g in range(1, 4):
             hx[own, e, g - 1 : g, :] = aux[g, e : e + 1, :]
@@ -197,11 +200,23 @@
 
     send(hx.at[own, 0], hsend.at[0], hrecv.at[0], plane)
     publish(0)
+    send(mine.at[1], psend.at[1], precv.at[1], column, piece.at[seat, 1])
+    for e in range(2, NB):
+
+        @pl.when(seat != e)
+        def _():
+            send(mine.at[e], psend.at[2], precv.at[2], [device(x, y, e // 4, e % 4)], piece.at[seat, 2])
+
     send(hx.at[own, pl.ds(1, NB - 1)], hsend.at[1], hrecv.at[1], plane)
     hx_first = hx.at[pl.ds(0, NOB - 1), 0]
     hx_rest = hx.at[pl.ds(0, NOB - 1), pl.ds(1, NB - 1)]
-    settle(late, precv.at[1])
-    pl.loop(1, NB)(unpack)
+    settle(piece.at[pl.ds(0, GRP - 1), 1], precv.at[1])
+    yo[1] = unpack(1)[0:K]
+
+    @pl.when(seat >= 2)
+    def _():
+        settle(piece.at[pl.ds(0, GRP - 1), 2], precv.at[2])
+        yo[seat] = unpack(2)[0:K]
 
     @pl.loop(0, NB)
     def _(e):
@@ -235,34 +250,27 @@
         copy.wait()
     settle(hx_first, hrecv.at[0])
 
-    def hand_over(e):
-        return pltpu.make_async_remote_copy(
-            src_ref=yo.at[e],
-            dst_ref=yx.at[e],
-            send_sem=ysend.at[e],
-            recv_sem=yrecv.at[e],
-            device_id=sibling,
-            device_id_type=MESH,
-        )
-
-    def one_level(unit):
-        c, l = unit // LEVD, unit % LEVD
-        block = x_ref[l]
-        low = (block - jnp.sum(block, axis=0, keepdims=True) * (1.0 / K)).astype(BF16)
-        covar = jnp.dot(abt[c], low, preferred_element_type=F32)
-        gain = covar.astype(BF16) * locv[c]
-        delta = jnp.concatenate(
-            [
-                (dch[c, :, i * 128 : (i + 1) * 128].astype(F32) * scl[c, l, i : i + 1, :]).astype(BF16)
-                for i in range(MAXB)
-            ],
-            axis=1,
-        )
-        x_ref[l] = block + jnp.dot(delta, gain, preferred_element_type=F32)
-
     def state_quad(quad):
+        c = quad // (LEVD // QUAD)
+        start = (quad % (LEVD // QUAD)) * QUAD
+        lows, results, gain = [], [], None
         for i in range(QUAD):
-            one_level(quad * QUAD + i)
+            block = x_ref[start + i]
+            lows.append((block - jnp.sum(block, axis=0, keepdims=True) * (1.0 / K)).astype(BF16))
+        for i in range(QUAD + 1):
+            before = gain
+            if i < QUAD:
+                covar = jnp.dot(abt[c], lows[i], preferred_element_type=F32)
+                gain = covar.astype(BF16) * locv[c]
+            if i > 0:
+                factors = [
+                    (dch[c, :, j * 128 : (j + 1) * 128].astype(F32) * scl[c, start + i - 1, j : j + 1, :]).astype(BF16)
+                    for j in range(MAXB)
+                ]
+                delta = jnp.concatenate(factors, axis=1)
+                results.append(jnp.dot(delta, before, preferred_element_type=F32))
+        for i in range(QUAD):
+            x_ref[start + i] += results[i]
 
     @pl.loop(0, NB)
     def _(c):
@@ -272,13 +280,13 @@
 
         @pl.when((c >= 1) & (c < NB - 1))
         def _():
-            @pl.when(core == (c + 1) % 2)
+            @pl.when(seat == c + 1)
             def _():
-                hand_over(c + 1).wait_send()
-
-            @pl.when(core != (c + 1) % 2)
+                settle(yx.at[pl.ds(0, GRP - 1)], ysend.at[c + 1])
+
+            @pl.when(seat != c + 1)
             def _():
-                hand_over(c + 1).wait_recv()
+                settle(yx.at[c + 1], yrecv.at[c + 1])
                 yo[c + 1] = yx[c + 1]
 
         @pl.when(c < NB - 1)
@@ -296,25 +304,32 @@
         rows[2] = COUPLE / variance
 
         take(c, ab, brecv)
-        for b in range(NOB):
-            low = (rows[0, b : b + 1, :] + rows[1, b : b + 1, :] * ab[c, b].astype(F32)).astype(BF16)
-            dyb[b] = low
-            dys[:, b * 128 : (b + 1) * 128] = (low.astype(F32) * rows[2, b : b + 1, :]).astype(BF16)
+
+        def increments():
+            for b in range(NOB):
+                low = (rows[0, b : b + 1, :] + rows[1, b : b + 1, :] * ab[c, b].astype(F32)).astype(BF16)
+                dyb[b] = low
+                dys[:, b * 128 : (b + 1) * 128] = (low.astype(F32) * rows[2, b : b + 1, :]).astype(BF16)
 
         @pl.when(c < NB - 1)
         def _():
+            increments()
             regress(c, c + 1)
             publish(c + 1)
 
-        @pl.loop(c + 2 + (c + core) % 2, NB, step=2)
-        def _(e):
-            transposed(e)
-            nearness(c, e)
-            regress(c, e)
-
-            @pl.when(e == c + 2)
+        @pl.when(c == NB - 1)
+        def _():
+            increments()
+
+        @pl.when((seat >= 2) & (seat >= c + 2))
+        def _():
+            transposed(seat)
+            nearness(c, seat)
+            regress(c, seat)
+
+            @pl.when(seat == c + 2)
             def _():
-                hand_over(e).start()
+                send(yo.at[seat], ysend.at[seat], yrecv.at[seat], column, yx.at[seat])
 
         abc[...] = ab[c]
         vhc[:, 0, :] = variance
@@ -331,16 +346,23 @@
             weight = jnp.where(i < used, SCOUPLE, 0.0) / theirs[0:1, :]
             scl[c, :, i, :] = weight / (1.0 + gap * gap)
 
-        first = jnp.where(c == 0, 0, 2 * c - 1)
-        last = jnp.where(c >= NB - 2, 2 * c + 2, 2 * c + 1)
-        pl.loop(jnp.where(c == NB - 1, 2 * c, first), last)(state_quad)
+        pl.loop(c * (LEVD // QUAD), (c + 1) * (LEVD // QUAD))(state_quad)
 
         final = yo[c] + dyb[own].astype(F32)
         yt[...] = jnp.transpose(final)
         post_ref[c] = yt[pl.ds(pl.multiple_of(seat * OWN, OWN), OWN), :]
 
-    settle(early, psend.at[0])
-    settle(late, psend.at[1])
+    settle(piece.at[pl.ds(0, GRP - 1), 0], psend.at[0])
+    settle(piece.at[pl.ds(0, GRP - 1), 1], psend.at[1])
+
+    @pl.when(seat >= 2)
+    def _():
+        settle(mine.at[pl.ds(0, NB - 3)], psend.at[2])
+
+    @pl.when(seat < 2)
+    def _():
+        settle(mine.at[pl.ds(0, NB - 2)], psend.at[2])
+
     settle(hx_first, hsend.at[0])
     settle(hx_rest, hsend.at[1])
 
@@ -367,7 +389,8 @@
             pltpu.VMEM((4, NB, OWN), F32),
             pltpu.SMEM((MAXB, 1, NB), jnp.int32),
             pltpu.SMEM((1, NB), jnp.int32),
-            pltpu.VMEM((GRP, 1 + NB, OWN, 128), F32),
+            pltpu.VMEM((NB, OWN, 128), F32),
+            pltpu.VMEM((GRP, 3, OWN, 128), F32),
             pltpu.VMEM((NB, K, 128), F32),
             pltpu.VMEM((NB, K, 128), F32),
             pltpu.VMEM((128, K), F32),
@@ -392,8 +415,8 @@
             pltpu.VMEM((NB, MAXB * 128, COLD), BF16),
             dma((9,)),
             dma((NB,)),
-            dma((2,)),
-            dma((2,)),
+            dma((3,)),
+            dma((3,)),
             dma((2,)),
             dma((2,)),
             dma((NB,)),

time: 76.9 us -> 69.7 us (0.906)
  Pallas kernels: 74.5 us -> 67.2 us
    pallas_call x1, Pallas kernels: 74.5 us -> 67.2 us  [per_device(): pl.pallas_call(kernel, out_shape=(jax.ShapeDtypeStruct((LEVD, K, COLD), F...]
where the time goes in v3:
time: 69.7 us; the launch traced here: 69.6 us
  Pallas kernels  67.2 us (96%)
  local copies, waits for them, and re-layouts  1.69 us (2%)
    pallas_call x1, Pallas kernels, per_device(): pl.pallas_call(kernel, out_shape=(jax.ShapeDtypeStruct((LEVD, K, COLD), F...  67.2 us
    unnamed x2, local copies, waits for them, and re-layouts  1.69 us

profile of v3, /device:TPU:0, one launch (start us, length us, event | category | flops | bytes accessed | tf_op | source)
XLA Modules:
  0.0 69.6 jit_solution(4484918215079667508)
XLA Ops:
  0.6 67.2 %shard_map.113 = (f32[8,80,512]{2,1,0:T(8,128)S(1)}, f32[8,16,80]{2,1,0:T(8,128)S(1)}) custom-call(f32[8,80,512]{2,1,0:T(8,128)} %state_hbm.1, f32[8,16,80]{2,1,0:T(8,128)} %bitcast.5, f32[8,16]{1,0:T(8,128)} %value_hbm.1, f32[8,16]{1,0:T(8,128)} %error_hbm.1, f32[8,16]{1,0:T(8,128)} %place_hbm.1, f32[8,16]{1,0:T(8,128)} %height_hbm.1, s32[6,1,8]{2,1,0:T(1,128)} %bitcast.6, ...), custom_call_target="tpu_custom_call" | custom-call | tf_op jit(solution)/shard_map/pallas_call | solution.py:379
  67.9 1.1 %copy.14 = f32[8,80,512]{2,1,0:T(8,128)} copy(f32[8,80,512]{2,1,0:T(8,128)S(1)} %get-tuple-element.8) | data formatting | bytes 2621440
  68.9 0.6 copy.15

commit v4 on v3

--- a/solution.py
+++ b/solution.py
@@ -32,6 +32,51 @@
 
 def device(x, y, core, z):
     return ((x * 4 + y) * 2 + core, z)
+
+
+def state_changes(x_ref, start, abt, dch, scl, loc, used=MAXB):
+    listed = slice(0, used * OBLK)
+    lows, results, gain = [], [], None
+    for i in range(QUAD):
+        block = x_ref[start + i]
+        lows.append((block - jnp.sum(block, axis=0, keepdims=True) * (1.0 / K)).astype(BF16))
+    for i in range(QUAD + 1):
+        before = gain
+        if i < QUAD:
+            covar = jnp.dot(abt[listed, :], lows[i], preferred_element_type=F32)
+            gain = covar.astype(BF16) * loc[listed, :]
+        if i > 0:
+            factors = [
+                (dch[:, j * 128 : (j + 1) * 128].astype(F32) * scl[start + i - 1, j : j + 1, :]).astype(BF16)
+                for j in range(used)
+            ]
+            delta = jnp.concatenate(factors, axis=1)
+            results.append(jnp.dot(delta, before, preferred_element_type=F32))
+    return results
+
+
+def last_kernel(x_ref, post_ref, abt, dch, scl, loc, x_hbm, post_hbm, held, out_sem, post_sem):
+    store_post = pltpu.make_async_copy(post_ref, post_hbm, post_sem)
+    store_post.start()
+
+    def store(l):
+        return pltpu.make_async_copy(held.at[l], x_hbm.at[l], out_sem.at[l])
+
+    count = jnp.max(scl[0, 7:8, :])
+    for used in range(1, MAXB + 1):
+
+        @pl.when((count > used - 0.5) & (count < used + 0.5))
+        def _():
+            @pl.loop(0, LEVD // QUAD)
+            def _(h):
+                results = state_changes(x_ref, h * QUAD, abt, dch, scl, loc, used)
+                for i in range(QUAD):
+                    held[h * QUAD + i] = x_ref[h * QUAD + i] + results[i]
+                    store(h * QUAD + i).start()
+
+    for l in range(LEVD):
+        store(l).wait()
+    store_post.wait()
 
 
 def kernel(
@@ -47,6 +92,10 @@
     mask_hbm,
     x_ref,
     post_ref,
+    abt_last,
+    dch_last,
+    scl_last,
+    loc_last,
     prior,
     vectors,
     blocks_ref,
@@ -129,8 +178,10 @@
     def load_loc(c):
         return pltpu.make_async_copy(loc_hbm.at[c], locv.at[c], loc_sem.at[c])
 
-    for c in range(NB):
+    load_last = pltpu.make_async_copy(loc_hbm.at[NB - 1], loc_last, loc_sem.at[NB - 1])
+    for c in range(NB - 1):
         load_loc(c).start()
+    load_last.start()
 
     for copy in small[:5]:
         copy.wait()
@@ -248,27 +299,13 @@
 
     for copy in small[6:]:
         copy.wait()
+    scl[NB - 1] = jnp.full((LEVD, 8, 128), counts_ref[0, NB - 1].astype(F32))
     settle(hx_first, hrecv.at[0])
 
     def state_quad(quad):
         c = quad // (LEVD // QUAD)
         start = (quad % (LEVD // QUAD)) * QUAD
-        lows, results, gain = [], [], None
-        for i in range(QUAD):
-            block = x_ref[start + i]
-            lows.append((block - jnp.sum(block, axis=0, keepdims=True) * (1.0 / K)).astype(BF16))
-        for i in range(QUAD + 1):
-            before = gain
-            if i < QUAD:
-                covar = jnp.dot(abt[c], lows[i], preferred_element_type=F32)
-                gain = covar.astype(BF16) * locv[c]
-            if i > 0:
-                factors = [
-                    (dch[c, :, j * 128 : (j + 1) * 128].astype(F32) * scl[c, start + i - 1, j : j + 1, :]).astype(BF16)
-                    for j in range(MAXB)
-                ]
-                delta = jnp.concatenate(factors, axis=1)
-                results.append(jnp.dot(delta, before, preferred_element_type=F32))
+        results = state_changes(x_ref, start, abt.at[c], dch.at[c], scl.at[c], locv.at[c])
         for i in range(QUAD):
             x_ref[start + i] += results[i]
 
@@ -334,7 +371,6 @@
         abc[...] = ab[c]
         vhc[:, 0, :] = variance
         vhc[:, 1, :] = hx[:, c, 2, :]
-        load_loc(c).wait()
         used = counts_ref[0, c]
         for i in range(MAXB):
             block = blocks_ref[i, 0, c]
@@ -346,12 +382,19 @@
             weight = jnp.where(i < used, SCOUPLE, 0.0) / theirs[0:1, :]
             scl[c, :, i, :] = weight / (1.0 + gap * gap)
 
-        pl.loop(c * (LEVD // QUAD), (c + 1) * (LEVD // QUAD))(state_quad)
+        @pl.when(c < NB - 1)
+        def _():
+            load_loc(c).wait()
+            pl.loop(c * (LEVD // QUAD), (c + 1) * (LEVD // QUAD))(state_quad)
 
         final = yo[c] + dyb[own].astype(F32)
         yt[...] = jnp.transpose(final)
         post_ref[c] = yt[pl.ds(pl.multiple_of(seat * OWN, OWN), OWN), :]
 
+    abt_last[...] = abt[NB - 1]
+    dch_last[...] = dch[NB - 1]
+    scl_last[...] = scl[NB - 1]
+    load_last.wait()
     settle(piece.at[pl.ds(0, GRP - 1), 0], psend.at[0])
     settle(piece.at[pl.ds(0, GRP - 1), 1], psend.at[1])
 
@@ -376,14 +419,18 @@
     vmem = pl.BlockSpec(memory_space=pltpu.VMEM)
     hbm = pl.BlockSpec(memory_space=pltpu.HBM)
     dma = pltpu.SemaphoreType.DMA
-    analysis, post = pl.pallas_call(
+    carried = pl.pallas_call(
         kernel,
         out_shape=(
             jax.ShapeDtypeStruct((LEVD, K, COLD), F32),
             jax.ShapeDtypeStruct((NB, OWN, K), F32),
+            jax.ShapeDtypeStruct((MAXB * 128, K), BF16),
+            jax.ShapeDtypeStruct((K, MAXB * 128), BF16),
+            jax.ShapeDtypeStruct((LEVD, 8, 128), F32),
+            jax.ShapeDtypeStruct((MAXB * 128, COLD), BF16),
         ),
         in_specs=[hbm] * 10,
-        out_specs=(vmem, vmem),
+        out_specs=(vmem,) * 6,
         scratch_shapes=[
             pltpu.VMEM((NB, OWN, K), F32),
             pltpu.VMEM((4, NB, OWN), F32),
@@ -412,7 +459,7 @@
             pltpu.VMEM((NB, MAXB * 128, K), BF16),
             pltpu.VMEM((NB, K, MAXB * 128), BF16),
             pltpu.VMEM((NB, LEVD, 8, 128), F32),
-            pltpu.VMEM((NB, MAXB * 128, COLD), BF16),
+            pltpu.VMEM((NB - 1, MAXB * 128, COLD), BF16),
             dma((9,)),
             dma((NB,)),
             dma((3,)),
@@ -427,7 +474,7 @@
             dma((NB,)),
         ],
         compiler_params=pltpu.CompilerParams(
-            collective_id=0, has_side_effects=True, vmem_limit_bytes=48 * 2**20
+            collective_id=0, has_side_effects=True, vmem_limit_bytes=32 * 2**20
         ),
     )(
         *(
@@ -446,6 +493,14 @@
             )
         )
     )
+    analysis, post = pl.pallas_call(
+        last_kernel,
+        out_shape=(pltpu.HBM((LEVD, K, COLD), F32), pltpu.HBM((NB, OWN, K), F32)),
+        in_specs=[vmem] * 6,
+        out_specs=(hbm, hbm),
+        scratch_shapes=[pltpu.VMEM((LEVD, K, COLD), F32), dma((LEVD,)), dma(())],
+        compiler_params=pltpu.CompilerParams(vmem_limit_bytes=32 * 2**20),
+    )(*carried)
     return analysis, jnp.swapaxes(post, 1, 2)
 
 

time: 69.7 us -> 67.8 us (0.973)
  local copies, waits for them, and re-layouts: 1.69 us -> 0 us
  Pallas kernels: 67.2 us -> 66.5 us
    pallas_call x1, Pallas kernels: 67.2 us -> 64.2 us  [per_device(): pl.pallas_call(kernel, out_shape=(jax.ShapeDtypeStruct((LEVD, K, COLD), F...]
    pallas_call x0 -> x1, Pallas kernels: none -> 2.29 us  [per_device(): pl.pallas_call(last_kernel, out_shape=(pltpu.HBM((LEVD, K, COLD), F32), p...]
    unnamed x2 -> x0, local copies, waits for them, and re-layouts: 1.69 us -> none
where the time goes in v4:
time: 67.8 us; the launch traced here: 67.2 us
  Pallas kernels  66.5 us (98%)
    pallas_call x1, Pallas kernels, per_device(): pl.pallas_call(kernel, out_shape=(jax.ShapeDtypeStruct((LEVD, K, COLD), F...  64.2 us
    pallas_call x1, Pallas kernels, per_device(): pl.pallas_call(last_kernel, out_shape=(pltpu.HBM((LEVD, K, COLD), F32), p...  2.29 us

profile of v4, /device:TPU:0, one launch (start us, length us, event | category | flops | bytes accessed | tf_op | source)
XLA Modules:
  0.0 67.2 jit_solution(17645928961941383441)
XLA Ops:
  0.6 64.2 %shard_map.113 = (f32[8,80,512]{2,1,0:T(8,128)S(1)}, f32[8,16,80]{2,1,0:T(8,128)S(1)}, bf16[768,80]{1,0:T(8,128)(2,1)S(1)}, bf16[80,768]{1,0:T(8,128)(2,1)S(1)},...) custom-call(f32[8,80,512]{2,1,0:T(8,128)} %state_hbm.1, f32[8,16,80]{2,1,0:T(8,128)} %bitcast.4, ...), custom_call_target="tpu_custom_call" | custom-call | tf_op jit(solution)/shard_map/pallas_call | solution.py:422
  64.9 2.3 %shard_map.114 = (f32[8,80,512]{2,1,0:T(8,128)}, f32[8,16,80]{2,1,0:T(8,128)}) custom-call(f32[8,80,512]{2,1,0:T(8,128)S(1)} %get-tuple-element.10.x_ref, f32[8,16,80]{2,1,0:T(8,128)S(1)} %get-tuple-element.11.post_ref, bf16[768,80]{1,0:T(8,128)(2,1)S(1)} %get-tuple-element.12.abt, bf16[80,768]{1,0:T(8,128)(2,1)S(1)} %get-tuple-element.13.dch, ...), custom_call_target="tpu_custom_call" | custom-call | tf_op jit(solution)/shard_map/pallas_call | solution.py:496

commit v5 on v4

--- a/solution.py
+++ b/solution.py
@@ -299,7 +299,7 @@
 
     for copy in small[6:]:
         copy.wait()
-    scl[NB - 1] = jnp.full((LEVD, 8, 128), counts_ref[0, NB - 1].astype(F32))
+    scl_last[...] = jnp.full((LEVD, 8, 128), counts_ref[0, NB - 1].astype(F32))
     settle(hx_first, hrecv.at[0])
 
     def state_quad(quad):
@@ -342,21 +342,22 @@
 
         take(c, ab, brecv)
 
-        def increments():
+        def increments(scaled):
             for b in range(NOB):
                 low = (rows[0, b : b + 1, :] + rows[1, b : b + 1, :] * ab[c, b].astype(F32)).astype(BF16)
                 dyb[b] = low
-                dys[:, b * 128 : (b + 1) * 128] = (low.astype(F32) * rows[2, b : b + 1, :]).astype(BF16)
+                if scaled:
+                    dys[:, b * 128 : (b + 1) * 128] = (low.astype(F32) * rows[2, b : b + 1, :]).astype(BF16)
 
         @pl.when(c < NB - 1)
         def _():
-            increments()
+            increments(True)
             regress(c, c + 1)
             publish(c + 1)
 
         @pl.when(c == NB - 1)
         def _():
-            increments()
+            increments(False)
 
         @pl.when((seat >= 2) & (seat >= c + 2))
         def _():
@@ -371,16 +372,25 @@
         abc[...] = ab[c]
         vhc[:, 0, :] = variance
         vhc[:, 1, :] = hx[:, c, 2, :]
-        used = counts_ref[0, c]
-        for i in range(MAXB):
-            block = blocks_ref[i, 0, c]
-            cut = slice(i * 128, (i + 1) * 128)
-            abt[c, cut, :] = jnp.transpose(abc[block].astype(F32)).astype(BF16)
-            dch[c, :, cut] = dyb[block]
-            theirs = vhc[block]
-            gap = (level - theirs[1:2, :]) * INV_VREACH
-            weight = jnp.where(i < used, SCOUPLE, 0.0) / theirs[0:1, :]
-            scl[c, :, i, :] = weight / (1.0 + gap * gap)
+        def prepare(turned, deltas, weights):
+            used = counts_ref[0, c]
+            for i in range(MAXB):
+                block = blocks_ref[i, 0, c]
+                cut = slice(i * 128, (i + 1) * 128)
+                turned[cut, :] = jnp.transpose(abc[block].astype(F32)).astype(BF16)
+                deltas[:, cut] = dyb[block]
+                theirs = vhc[block]
+                gap = (level - theirs[1:2, :]) * INV_VREACH
+                weight = jnp.where(i < used, SCOUPLE, 0.0) / theirs[0:1, :]
+                weights[:, i, :] = weight / (1.0 + gap * gap)
+
+        @pl.when(c == NB - 1)
+        def _():
+            prepare(abt_last, dch_last, scl_last)
+
+        @pl.when(c < NB - 1)
+        def _():
+            prepare(abt.at[c], dch.at[c], scl.at[c])
 
         @pl.when(c < NB - 1)
         def _():
@@ -391,9 +401,6 @@
         yt[...] = jnp.transpose(final)
         post_ref[c] = yt[pl.ds(pl.multiple_of(seat * OWN, OWN), OWN), :]
 
-    abt_last[...] = abt[NB - 1]
-    dch_last[...] = dch[NB - 1]
-    scl_last[...] = scl[NB - 1]
     load_last.wait()
     settle(piece.at[pl.ds(0, GRP - 1), 0], psend.at[0])
     settle(piece.at[pl.ds(0, GRP - 1), 1], psend.at[1])

time: 67.8 us -> 68.5 us (1.010); the launches traced: 67.2 us -> 68.9 us
  Pallas kernels: 66.5 us -> 68.2 us
    pallas_call x1, Pallas kernels: 2.29 us -> 4.11 us  [per_device(): pl.pallas_call(last_kernel, out_shape=(pltpu.HBM((LEVD, K, COLD), F32), p...]
where the time goes in v5:
time: 68.5 us; the launch traced here: 68.9 us
  Pallas kernels  68.2 us (100%)
    pallas_call x1, Pallas kernels, per_device(): pl.pallas_call(kernel, out_shape=(jax.ShapeDtypeStruct((LEVD, K, COLD), F...  64.1 us
    pallas_call x1, Pallas kernels, per_device(): pl.pallas_call(last_kernel, out_shape=(pltpu.HBM((LEVD, K, COLD), F32), p...  4.11 us

profile of v5, /device:TPU:0, one launch (start us, length us, event | category | flops | bytes accessed | tf_op | source)
XLA Modules:
  0.0 68.9 jit_solution(4921432393260924871)
XLA Ops:
  0.6 64.1 %shard_map.113 = (f32[8,80,512]{2,1,0:T(8,128)S(1)}, f32[8,16,80]{2,1,0:T(8,128)S(1)}, bf16[768,80]{1,0:T(8,128)(2,1)S(1)}, bf16[80,768]{1,0:T(8,128)(2,1)S(1)},...) custom-call(f32[8,80,512]{2,1,0:T(8,128)} %state_hbm.1, f32[8,16,80]{2,1,0:T(8,128)} %bitcast.4, ...), custom_call_target="tpu_custom_call" | custom-call | tf_op jit(solution)/shard_map/pallas_call | solution.py:429
  64.8 4.1 %shard_map.114 = (f32[8,80,512]{2,1,0:T(8,128)}, f32[8,16,80]{2,1,0:T(8,128)}) custom-call(f32[8,80,512]{2,1,0:T(8,128)S(1)} %get-tuple-element.10.x_ref, f32[8,16,80]{2,1,0:T(8,128)S(1)} %get-tuple-element.11.post_ref, bf16[768,80]{1,0:T(8,128)(2,1)S(1)} %get-tuple-element.12.abt, bf16[80,768]{1,0:T(8,128)(2,1)S(1)} %get-tuple-element.13.dch, ...), custom_call_target="tpu_custom_call" | custom-call | tf_op jit(solution)/shard_map/pallas_call | solution.py:503
